TPU v7x, 256 devices: a whole 4x4x8 slice. The times are simulated.
256 devices in a mesh: seq: 32 (over z, x), exp: 8 (over y, core).
Axes of the slice: x: 4, y: 4, z: 8, core: 2. Of those that a mesh axis runs over, the one named last changes fastest.
Arguments:
- mixer_input: bfloat16 [2048, 8192], P('seq', 'exp'), may hold values from -6 to 6
- gate_input: bfloat16 [2048, 8192], P('seq', 'exp'), may hold values from -6 to 6
- conv_weight: bfloat16 [4, 8192], P(None, 'exp'), may hold values from -3 to 3
- conv_bias: float32 [8192], P('exp'), may hold values from -3 to 3
- rank_weight: bfloat16 [8192, 256], P('exp'), may hold values from -0.0625 to 0.0625
- state_weight: bfloat16 [8192, 32], P('exp'), may hold values from -0.03125 to 0.03125
- delta_weight: bfloat16 [256, 8192], P(None, 'exp'), may hold values from -0.375 to 0.375
- delta_bias: float32 [8192], P('exp'), may hold values from -1 to 1
- log_rates: float32 [16, 8192], P(None, 'exp'), may hold values from -10 to -1
- skip_gain: float32 [8192], P('exp'), may hold values from 0.5 to 1.5
- out_proj: bfloat16 [8192, 4096], P('exp', 'seq'), may hold values from -0.0625 to 0.0625
- residual: bfloat16 [2048, 4096], P(('seq', 'exp')), may hold values from -3 to 3
- norm_gain: float32 [4096], replicated, may hold values from 0.5 to 1.5
- router: float32 [4096, 8], replicated, may hold values from -0.09375 to 0.09375
- w_gate: bfloat16 [8, 4096, 14336], P('exp', None, 'seq'), may hold values from -0.09375 to 0.09375
- w_up: bfloat16 [8, 4096, 14336], P('exp', None, 'seq'), may hold values from -0.09375 to 0.09375
- w_down: bfloat16 [8, 14336, 4096], P('exp', 'seq'), may hold values from -0.09375 to 0.09375
- routes: int32 [2048, 2], P(('seq', 'exp')), may hold values from 0 to 7, all different within a row; in each aligned block of 8 rows (0 to 7, 8 to 15, ...) at most 4 rows name the same one
Outputs:
- layer_out: bfloat16 [2048, 4096], P(('seq', 'exp'))
- expert_mix: float32 [2048, 4096], P(('seq', 'exp'))
Inputs may be any that keep to these rules, and one draw needn't show every extreme that they name: `routes`: each row names two different experts; among the 8 rows of one device no expert is named more than 4 times, a bound that some block reaches there on some device.
All inputs are finite; a program needn't handle non-finite values.
Results may differ from a plain program's by a relative error of at most 0.024.
Values may be sent and summed in bfloat16 or wider, within the bound.
No kernel may reach another device: no remote copies, remote signals or barrier semaphores. Data moves between devices by JAX's collectives and lax.ppermute only.
A program may use at most 128 MiB of HBM per device.

v0:
```python
import jax
import jax.numpy as jnp
from jax import lax
from jax.sharding import PartitionSpec as P


def shifted(block, axis, distance):
    devices = range(lax.axis_size(axis))
    route = [(i - distance, i) for i in devices if i - distance in devices]
    return lax.ppermute(block, axis, route)


def entering(array, axis, combine, identity):
    count, index = (lax.axis_size(axis), lax.axis_index(axis))
    everything = jax.tree.map(lambda part: lax.all_gather(part, axis), array)
    start = jax.tree.map(
        lambda part, zero: jnp.broadcast_to(jnp.asarray(zero, part.dtype), part.shape),
        array,
        identity,
    )

    def hop(k, before):
        reached = k < index
        new = combine(before, jax.tree.map(lambda part: part[k], everything))
        return jax.tree.map(lambda a, b: jnp.where(reached, a, b), new, before)

    return lax.fori_loop(0, count, hop, start)


def combine_pair(earlier, following):
    return (earlier[0] * following[0], following[0] * earlier[1] + following[1])


def body(
    mixer_input,
    gate_input,
    conv_weight,
    conv_bias,
    rank_weight,
    state_weight,
    delta_weight,
    delta_bias,
    log_rates,
    skip_gain,
    out_proj,
    residual,
    norm_gain,
    router,
    w_gate,
    w_up,
    w_down,
    routes,
):
    taps = conv_weight.shape[0]
    block_rows = mixer_input.shape[0]
    rim_rows = shifted(mixer_input[block_rows - (taps - 1) :], "seq", 1)
    padded = jnp.concatenate([rim_rows, mixer_input], axis=0)
    conv_sum = jnp.zeros(mixer_input.shape, jnp.float32) + conv_bias[None, :]
    for offset in range(taps):
        conv_sum = conv_sum + conv_weight[offset].astype(jnp.float32)[None, :] * padded[
            offset : offset + block_rows
        ].astype(jnp.float32)
    conv_act = jax.nn.silu(conv_sum).astype(jnp.bfloat16)
    delta_part = jnp.dot(conv_act, rank_weight, preferred_element_type=jnp.float32)
    state_part = jnp.dot(conv_act, state_weight, preferred_element_type=jnp.float32)
    delta_sum, state_maps = lax.psum((delta_part, state_part), "exp")
    delta_low = delta_sum.astype(jnp.bfloat16)
    states = log_rates.shape[0]
    input_map = state_maps[:, :states]
    output_map = state_maps[:, states:]
    delta = jax.nn.softplus(
        jnp.dot(delta_low, delta_weight, preferred_element_type=jnp.float32) + delta_bias[None, :]
    )
    decay_rate = jnp.exp(log_rates)
    conv_float = conv_act.astype(jnp.float32)
    driven = (delta * conv_float)[:, None, :] * input_map[:, :, None]
    decays = jnp.exp(-delta[:, None, :] * decay_rate[None])
    passed = jnp.cumsum(delta, axis=0)
    total_dt = passed[-1]
    weights_left = jnp.exp(-(total_dt[None, :] - passed)[:, None, :] * decay_rate[None])
    transform = (jnp.exp(-total_dt[None, :] * decay_rate), jnp.sum(weights_left * driven, axis=0))
    incoming = entering(
        transform, "seq", combine_pair, (jnp.ones_like(decay_rate), jnp.zeros_like(decay_rate))
    )
    start_state = incoming[1]

    def advance(carried, inputs):
        decay_t, driven_t, output_t = inputs
        carried = decay_t * carried + driven_t
        return (carried, jnp.sum(output_t[:, None] * carried, axis=0))

    last_state, scan_out = lax.scan(advance, start_state, (decays, driven, output_map))
    scan_out = scan_out + skip_gain[None, :] * conv_float
    gated = (scan_out * jax.nn.silu(gate_input.astype(jnp.float32))).astype(jnp.bfloat16)
    tok_dev = residual.shape[0]
    partial_value = jnp.dot(
        gated,
        lax.all_gather(out_proj, "seq", axis=1, tiled=True),
        preferred_element_type=jnp.float32,
    )
    mamba_out = lax.psum_scatter(partial_value, "exp", scatter_dimension=0, tiled=True)
    hidden = residual.astype(jnp.float32) + mamba_out
    mean_square = jnp.mean(hidden * hidden, axis=1, keepdims=True)
    normed = (hidden * lax.rsqrt(mean_square + 1e-05) * norm_gain[None, :]).astype(jnp.bfloat16)
    logits = jnp.dot(normed.astype(jnp.float32), router, precision=lax.Precision.HIGHEST)
    experts = router.shape[1]
    expert_ids = jnp.arange(experts, dtype=jnp.int32)
    matches = (routes[:, :, None] == expert_ids[None, None, :]).astype(jnp.float32)
    chosen = jnp.sum(matches * logits[:, None, :], axis=2)
    route_weights = jax.nn.sigmoid(chosen - chosen[:, ::-1])
    capacity = max(2, 4 * tok_dev // experts)
    flat_ids = routes.reshape(-1)
    route_pos = jnp.arange(flat_ids.shape[0], dtype=jnp.int32)
    earlier_same = (flat_ids[:, None] == flat_ids[None, :]) & (
        route_pos[None, :] < route_pos[:, None]
    )
    slot_rank = jnp.sum(earlier_same.astype(jnp.int32), axis=1)
    slot_of = flat_ids * capacity + slot_rank
    slot_ids = jnp.arange(experts * capacity, dtype=jnp.int32)
    placing = (slot_ids[:, None] == slot_of[None, :]).astype(jnp.bfloat16)
    repeated = jnp.repeat(normed, 2, axis=0)
    outbound = jnp.dot(placing, repeated, preferred_element_type=jnp.float32).astype(jnp.bfloat16)
    arrived = lax.all_to_all(outbound, "exp", split_axis=0, concat_axis=0, tiled=True)
    gate_local = w_gate[0]
    up_local = w_up[0]
    down_local = w_down[0]
    shard_part = lax.all_gather(arrived, "seq", axis=0, tiled=True)
    gate_part = jnp.dot(shard_part, gate_local, preferred_element_type=jnp.float32)
    up_part = jnp.dot(shard_part, up_local, preferred_element_type=jnp.float32)
    activated = (jax.nn.silu(gate_part) * up_part).astype(jnp.bfloat16)
    expert_out = lax.psum_scatter(
        jnp.dot(activated, down_local, preferred_element_type=jnp.float32).astype(jnp.bfloat16),
        "seq",
        scatter_dimension=0,
        tiled=True,
    ).astype(jnp.float32)
    returned = lax.all_to_all(expert_out, "exp", split_axis=0, concat_axis=0, tiled=True)
    picked = jnp.take(returned, slot_of, axis=0)
    moe_sum = jnp.sum(picked.reshape(tok_dev, 2, -1) * route_weights[:, :, None], axis=1)
    return ((hidden + moe_sum).astype(jnp.bfloat16), moe_sum)


def solution(mesh):
    in_specs = (
        P("seq", "exp"),
        P("seq", "exp"),
        P(None, "exp"),
        P("exp"),
        P("exp", None),
        P("exp", None),
        P(None, "exp"),
        P("exp"),
        P(None, "exp"),
        P("exp"),
        P("exp", "seq"),
        P(("seq", "exp"), None),
        P(),
        P(),
        P("exp", None, "seq"),
        P("exp", None, "seq"),
        P("exp", "seq", None),
        P(("seq", "exp"), None),
    )
    out_specs = (P(("seq", "exp"), None), P(("seq", "exp"), None))
    return jax.shard_map(body, mesh=mesh, in_specs=in_specs, out_specs=out_specs, check_vma=False)
```

profile of v0, /device:TPU:1, one launch (start us, length us, event | category | flops | bytes accessed | tf_op | source)
XLA Modules:
  0.0 738.1 jit_solution(16103797339628601987)
XLA Ops:
  8.0 3.9 collective-permute-start
  12.8 1.4 multiply_convert_fusion.1
  14.2 1.2 fusion.34
  15.4 1.0 fusion.35
  16.4 23.9 %all-reduce = (bf16[64,256]{1,0:T(8,128)(2,1)S(1)}, f32[64,32]{0,1:T(8,128)S(1)}) all-reduce(f32[64,256]{1,0:T(8,128)S(1)} %fusion.34, f32[64,32]{0,1:T(8,128)S(1)} %fusion.35), channel_id=1, replica_groups=mesh['seq'=32,'exp'=8] {'exp'}, use_global_device_ids=true, to_apply=%region_0.1 | all-reduce | flops 18432 | bytes 114688 | tf_op jit(solution)/shard_map/psum | solution.py:66
  40.3 1.0 fusion.30
  41.7 1.5 fusion.32
  43.2 4.3 broadcast_multiply_fusion
  49.2 77.0 %all-gather.13.cloned.1.call-done = f32[512,1024]{1,0:T(8,128)} async-done(((f32[16,1024]{1,0:T(8,128)}), f32[512,1024]{1,0:T(8,128)}) %all-gather.13.cloned.1.call-update) | async-done | bytes 2097168 | tf_op jit(solution)/shard_map/all_gather | solution.py:15
  126.2 78.3 %all-gather.11.cloned.1.call-done = f32[512,1024]{1,0:T(8,128)} async-done(((f32[16,1024]{1,0:T(8,128)}), f32[512,1024]{1,0:T(8,128)}) %all-gather.11.cloned.1.call-update) | async-done | bytes 2097168 | tf_op jit(solution)/shard_map/all_gather | solution.py:15
  204.5 30.0 %while.29 = (s32[]{:T(128)}, f32[16,1024]{1,0:T(8,128)S(1)}, s32[]{:T(128)}, f32[32,16,1024]{2,1,0:T(8,128)}, f32[32,16,1024]{2,1,0:T(8,128)}) while((s32[]{:T(128)}, f32[16,1024]{1,0:T(8,128)S(1)}, s32[]{:T(128)}, f32[32,16,1024]{2,1,0:T(8,128)}, f32[32,16,1024]{2,1,0:T(8,128)}) %tuple.91), condition=%wide.region_5.6_spmd.clone.clone, body=%wide.region_4.5_spmd.clone.sunk.clone | while | flops 65540 | bytes 262229 | solution.py:27
  234.5 71.4 %while.28 = (s32[]{:T(128)}, f32[16,1024]{1,0:T(8,128)S(1)}, f32[64,1024]{1,0:T(8,128)S(1)}, f32[64,16,1024]{2,1,0:T(8,128)}, f32[64,16,1024]{2,1,0:T(8,128)}, /*index=5*/f32[64,16]{1,0:T(8,128)S(1)}) while((s32[]{:T(128)}, f32[16,1024]{1,0:T(8,128)S(1)}, f32[64,1024]{1,0:T(8,128)S(1)}, f32[64,16,1024]{2,1,0:T(8,128)}, ...), condition=%wide.region_8.9_spmd.clone, body=%wide.region_6.8_spmd.sunk.clone | while | flops 64514 | bytes 274705 | solution.py:92
  260.2 1.0 multiply_reduce_fusion.6
  261.3 1.0 multiply_reduce_fusion.6
  275.8 1.0 multiply_reduce_fusion.6
  278.1 1.0 multiply_reduce_fusion.6
  279.2 1.0 multiply_reduce_fusion.6
  291.5 1.0 multiply_reduce_fusion.6
  292.6 1.0 multiply_reduce_fusion.6
  306.0 3.2 all-gather.7.cloned.1.call-done
  309.2 6.1 fusion.20
  315.7 32.0 %reduce-scatter.3.cloned.1.call-done = f32[8,4096]{1,0:T(8,128)} async-done(((f32[64,4096]{1,0:T(8,128)}), f32[8,4096]{1,0:T(8,128)}) %reduce-scatter.3.cloned.1.call-update) | async-done | bytes 131088 | tf_op jit(solution)/shard_map/reduce_scatter | solution.py:101
  347.7 1.1 multiply_reduce_fusion.3
  348.8 1.0 multiply_convert_fusion.2
  350.2 12.0 %all_to_all.28 = bf16[8,4,4096]{2,1,0:T(4,128)(2,1)S(1)} all-to-all(bf16[8,4,4096]{2,1,0:T(4,128)(2,1)S(1)} %all_to_all.18), channel_id=1, replica_groups=mesh['seq'=32,'exp'=8] {'exp'}, dimensions={0} | all-to-all | bytes 524288 | tf_op jit(solution)/shard_map/all_to_all | solution.py:123
  363.3 97.7 %all-gather.9.cloned.1.call-done = bf16[1024,4096]{1,0:T(8,128)(2,1)} async-done(((bf16[32,4096]{1,0:T(8,128)(2,1)}), bf16[1024,4096]{1,0:T(8,128)(2,1)}) %all-gather.9.cloned.1.call-update) | async-done | bytes 8388624 | tf_op jit(solution)/shard_map/all_gather | solution.py:127
  460.9 9.7 %fusion.5 = f32[1024,448]{0,1:T(8,128)} fusion(bf16[1024,4096]{1,0:T(8,128)(2,1)} %all-gather.9.cloned.1.call-done, bf16[1,4096,448]{1,2,0:T(8,128)(2,1)} %param.36), kind=kOutput, calls=%fused_computation.16 | convolution fusion | flops 3758096384 | bytes 13893632 | tf_op jit(solution)/shard_map/dot_general | solution.py:128
  470.6 15.4 %convolution_convert_fusion = bf16[1024,4096]{1,0:T(8,128)(2,1)} fusion(bf16[1,448,4096]{2,1,0:T(8,128)(2,1)} %param.38, f32[1024,448]{0,1:T(8,128)} %fusion.5, bf16[1024,4096]{1,0:T(8,128)(2,1)} %all-gather.9.cloned.1.call-done, bf16[1,4096,448]{1,2,0:T(8,128)(2,1)} %param.37), kind=kOutput, calls=%fused_computation.9 | convolution fusion | flops 7523139584 | bytes 25952256 | tf_op jit(solution)/shard_map/dot_general | solution.py:132
  486.3 222.6 %reduce-scatter.5.cloned.1.call-done = bf16[32,4096]{1,0:T(8,128)(2,1)} async-done(((bf16[1024,4096]{1,0:T(8,128)(2,1)}), bf16[32,4096]{1,0:T(8,128)(2,1)}) %reduce-scatter.5.cloned.1.call-update) | async-done | bytes 262160 | tf_op jit(solution)/shard_map/reduce_scatter | solution.py:131
  708.9 1.9 reshape.112
  710.8 8.9 %all-to-all-start.1 = ((f32[8,4,4096]{2,1,0:T(4,128)}), f32[8,4,4096]{2,1,0:T(4,128)S(1)}, u32[]{:S(2)}, u32[]{:S(2)}) async-start(f32[8,4,4096]{2,1,0:T(4,128)} %reshape.112), calls=%async_computation.3 | async-start | bytes 1048576 | tf_op jit(solution)/shard_map/all_to_all | solution.py:137
  720.2 9.0 %all-to-all-done.1 = f32[8,4,4096]{2,1,0:T(4,128)S(1)} async-done(((f32[8,4,4096]{2,1,0:T(4,128)}), f32[8,4,4096]{2,1,0:T(4,128)S(1)}, u32[]{:S(2)}, u32[]{:S(2)}) %all-to-all-start.1) | async-done | bytes 524320 | tf_op jit(solution)/shard_map/all_to_all | solution.py:137
  (284 shorter events, 100.2 us)
Async XLA Ops:
  7.2 33.1 %copy-start = (bf16[256,1024]{1,0:T(8,128)(2,1)S(1)}, bf16[256,1024]{1,0:T(8,128)(2,1)}, u32[]{:S(2)}) copy-start(bf16[256,1024]{1,0:T(8,128)(2,1)} %param.28) | copy-start | bytes 1572868
  7.2 119.0 %all-gather.13.cloned.1.call-start = ((), (), s32[]{:S(2)}) async-start(), calls=%async_computation.9 | async-start | bytes 2162688 | tf_op jit(solution)/shard_map/all_gather | solution.py:15
  8.0 4.8 collective-permute-start
  43.2 265.9 %copy-start.4 = (bf16[64,1024]{1,0:T(8,128)(2,1)S(1)}, bf16[64,1024]{1,0:T(8,128)(2,1)}, u32[]{:S(2)}) copy-start(bf16[64,1024]{1,0:T(8,128)(2,1)} %param.23) | copy-start | bytes 393220
  43.2 265.9 %copy-start.6 = (f32[1024]{0:T(1024)S(1)}, f32[1024]{0:T(1024)}, u32[]{:S(2)}) copy-start(f32[1024]{0:T(1024)} %param.31) | copy-start | bytes 12292
  47.6 157.0 %all-gather.11.cloned.1.call-start = ((), (), s32[]{:S(2)}) async-start(), calls=%async_computation.8 | async-start | bytes 2162688 | tf_op jit(solution)/shard_map/all_gather | solution.py:15
  48.3 260.9 %all-gather.7.cloned.1.call-start = ((), (), s32[]{:S(2)}) async-start(), calls=%async_computation.4 | async-start | bytes 8650752 | tf_op jit(solution)/shard_map/all_gather | solution.py:98
  49.0 298.7 %reduce-scatter.3.cloned.1.call-start = ((), (), s32[]{:S(2)}) async-start(), calls=%async_computation.5 | async-start | bytes 1179648 | tf_op jit(solution)/shard_map/reduce_scatter | solution.py:101
  309.2 6.2 copy-start.8
  309.2 38.5 %copy-start.2 = (bf16[8,4096]{1,0:T(8,128)(2,1)S(1)}, bf16[8,4096]{1,0:T(8,128)(2,1)}, u32[]{:S(2)}) copy-start(bf16[8,4096]{1,0:T(8,128)(2,1)} %param.33) | copy-start | bytes 196612
  309.2 39.6 %copy-start.7 = (f32[4096]{0:T(1024)S(1)}, f32[4096]{0:T(1024)}, u32[]{:S(2)}) copy-start(f32[4096]{0:T(1024)} %param.34) | copy-start | bytes 49156
  315.3 145.7 %all-gather.9.cloned.1.call-start = ((), (), s32[]{:S(2)}) async-start(), calls=%async_computation.6 | async-start | bytes 8650752 | tf_op jit(solution)/shard_map/all_gather | solution.py:127
  363.1 345.9 %reduce-scatter.5.cloned.1.call-start = ((), (), s32[]{:S(2)}) async-start(), calls=%async_computation.7 | async-start | bytes 8650752 | tf_op jit(solution)/shard_map/reduce_scatter | solution.py:131
  486.0 233.6 %copy-start.5 = (f32[4096,8]{0,1:T(8,128)S(1)}, f32[4096,8]{0,1:T(8,128)}, u32[]{:S(2)}) copy-start(f32[4096,8]{0,1:T(8,128)} %param.35) | copy-start | bytes 393220
  486.1 244.5 %copy-start.1 = (f32[8,4096]{1,0:T(8,128)S(1)}, f32[8,4096]{1,0:T(8,128)}, u32[]{:S(2)}) copy-start(f32[8,4096]{1,0:T(8,128)} %reduce-scatter.3.cloned.1.call-done) | copy-start | bytes 393220
  710.8 18.3 %all-to-all-start.1 = ((f32[8,4,4096]{2,1,0:T(4,128)}), f32[8,4,4096]{2,1,0:T(4,128)S(1)}, u32[]{:S(2)}, u32[]{:S(2)}) async-start(f32[8,4,4096]{2,1,0:T(4,128)} %reshape.112), calls=%async_computation.3 | async-start | bytes 1048576 | tf_op jit(solution)/shard_map/all_to_all | solution.py:137
  730.6 0.7 copy-start.3
Sparse Core Ops, SparseCore 0:
  47.7 78.5 all-gather.12
  129.4 75.1 all-gather.10
  207.0 102.1 all-gather.6
  315.4 32.2 reduce-scatter.2
  363.2 97.7 all-gather.8
  486.2 222.6 reduce-scatter.4
where the time goes:
time: 743 us; the launch traced here: 738 us
  waiting for transfers between devices  521 us (70%)
  other arithmetic  103 us (14%)
  blocking collectives  35.9 us (5%)
  matrix products  34.8 us (5%)
  between operations  14.4 us (2%)
  starting transfers between devices  13.2 us (2%)
  local copies, waits for them, and re-layouts  13 us (2%)
    reduce_scatter x1, waiting for transfers between devices, body(): lax.psum_scatter(jnp.dot(activated, down_local, preferred_element_type=jn...  223 us
    all_gather x2, waiting for transfers between devices, entering(): everything = jax.tree.map(lambda part: lax.all_gather(part, axis), array)  155 us
    all_gather x1, waiting for transfers between devices, body(): shard_part = lax.all_gather(arrived, 'seq', axis=0, tiled=True)  97.7 us
    reduce_sum x64, other arithmetic, advance(): return (carried, jnp.sum(output_t[:, None] * carried, axis=0))  61.7 us
    reduce_scatter x1, waiting for transfers between devices, body(): lax.psum_scatter(partial_value, 'exp', scatter_dimension=0, tiled=True)  32 us
    select_n x32, other arithmetic, hop(): return jax.tree.map(lambda a, b: jnp.where(reached, a, b), new, before)  29.3 us
    psum x1, blocking collectives, body(): delta_sum, state_maps = lax.psum((delta_part, state_part), 'exp')  23.9 us
    dot_general x1, matrix products, body(): jnp.dot(activated, down_local, preferred_element_type=jnp.float32)  15.4 us
  transfers between devices with their start and end apart: 8, of which 7 were waited for; matrix products, arithmetic and copies ran while one was open for 14% of the time, Pallas kernels for 0%

commit v1 on v0

--- a/solution.py
+++ b/solution.py
@@ -124,7 +124,14 @@
     gate_local = w_gate[0]
     up_local = w_up[0]
     down_local = w_down[0]
-    shard_part = lax.all_gather(arrived, "seq", axis=0, tiled=True)
+    ways, here, step = (lax.axis_size("seq"), lax.axis_index("seq"), arrived.shape[0])
+    line, have = (arrived, 1)
+    while have < ways:
+        line = jnp.concatenate(
+            [line, lax.ppermute(line, "seq", [(d, (d - have) % ways) for d in range(ways)])], axis=0
+        )
+        have = 2 * have
+    shard_part = jnp.roll(line, here * step, axis=0)
     gate_part = jnp.dot(shard_part, gate_local, preferred_element_type=jnp.float32)
     up_part = jnp.dot(shard_part, up_local, preferred_element_type=jnp.float32)
     activated = (jax.nn.silu(gate_part) * up_part).astype(jnp.bfloat16)

time: 743 us -> 984 us (1.32)
  waiting for transfers between devices: 521 us -> 727 us
  local copies, waits for them, and re-layouts: 13 us -> 34.8 us
  starting transfers between devices: 13.2 us -> 28.4 us
    ppermute x0 -> x5, waiting for transfers between devices: none -> 275 us  [body(): lax.ppermute(line, 'seq', [(d, (d - have) % ways) for d in range(ways)])]
    all_gather x1 -> x0, waiting for transfers between devices: 97.7 us -> none  [body(): shard_part = lax.all_gather(arrived, 'seq', axis=0, tiled=True)]
    reduce_scatter x1, waiting for transfers between devices: 223 us -> 255 us  [body(): lax.psum_scatter(jnp.dot(activated, down_local, preferred_element_type=jn...]
    ppermute x0 -> x5, starting transfers between devices: none -> 15.4 us  [body(): lax.ppermute(line, 'seq', [(d, (d - have) % ways) for d in range(ways)])]
    unnamed x19 -> x37, local copies, waits for them, and re-layouts: 0.13 us -> 15.3 us
  transfers between devices with their start and end apart: 8 -> 12, of which waited for: 7 -> 11; matrix products, arithmetic and copies ran while one was open for 14% -> 11% of each run, Pallas kernels for 0% -> 0%
where the time goes in v1:
time: 984 us; the launch traced here: 979 us
  waiting for transfers between devices  727 us (74%)
  other arithmetic  103 us (10%)
  blocking collectives  35.9 us (4%)
  local copies, waits for them, and re-layouts  34.8 us (4%)
  matrix products  33.1 us (3%)
  starting transfers between devices  28.4 us (3%)
  between operations  14.1 us (1%)
    ppermute x5, waiting for transfers between devices, body(): lax.ppermute(line, 'seq', [(d, (d - have) % ways) for d in range(ways)])  275 us
    reduce_scatter x1, waiting for transfers between devices, body(): lax.psum_scatter(jnp.dot(activated, down_local, preferred_element_type=jn...  255 us
    all_gather x2, waiting for transfers between devices, entering(): everything = jax.tree.map(lambda part: lax.all_gather(part, axis), array)  152 us
    reduce_sum x64, other arithmetic, advance(): return (carried, jnp.sum(output_t[:, None] * carried, axis=0))  61.6 us
    reduce_scatter x1, waiting for transfers between devices, body(): lax.psum_scatter(partial_value, 'exp', scatter_dimension=0, tiled=True)  32.4 us
    select_n x32, other arithmetic, hop(): return jax.tree.map(lambda a, b: jnp.where(reached, a, b), new, before)  29.3 us
    psum x1, blocking collectives, body(): delta_sum, state_maps = lax.psum((delta_part, state_part), 'exp')  23.9 us
  transfers between devices with their start and end apart: 12, of which 11 were waited for; matrix products, arithmetic and copies ran while one was open for 11% of the time, Pallas kernels for 0%

profile of v1, /device:TPU:1, one launch (start us, length us, event | category | flops | bytes accessed | tf_op | source)
XLA Modules:
  0.0 979.0 jit_solution(15519813588085259005)
XLA Ops:
  8.0 3.9 collective-permute-start
  16.5 23.9 %all-reduce = (bf16[64,256]{1,0:T(8,128)(2,1)S(1)}, f32[64,32]{0,1:T(8,128)S(1)}) all-reduce(f32[64,256]{1,0:T(8,128)S(1)} %fusion.42, f32[64,32]{0,1:T(8,128)S(1)} %fusion.43), channel_id=1, replica_groups=mesh['seq'=32,'exp'=8] {'exp'}, use_global_device_ids=true, to_apply=%region_0.1 | all-reduce | flops 18432 | bytes 114688 | tf_op jit(solution)/shard_map/psum | solution.py:66
  41.7 1.5 fusion.40
  43.4 4.3 broadcast_multiply_fusion
  48.7 73.2 %all-gather.8.cloned.1.call-done = f32[512,1024]{1,0:T(8,128)} async-done(((f32[16,1024]{1,0:T(8,128)}), f32[512,1024]{1,0:T(8,128)}) %all-gather.8.cloned.1.call-update) | async-done | bytes 2097168 | tf_op jit(solution)/shard_map/all_gather | solution.py:15
  121.9 78.3 %all-gather.10.cloned.1.call-done = f32[512,1024]{1,0:T(8,128)} async-done(((f32[16,1024]{1,0:T(8,128)}), f32[512,1024]{1,0:T(8,128)}) %all-gather.10.cloned.1.call-update) | async-done | bytes 2097168 | tf_op jit(solution)/shard_map/all_gather | solution.py:15
  200.2 30.0 %while.29 = (s32[]{:T(128)}, f32[16,1024]{1,0:T(8,128)S(1)}, s32[]{:T(128)}, f32[32,16,1024]{2,1,0:T(8,128)}, f32[32,16,1024]{2,1,0:T(8,128)}) while((s32[]{:T(128)}, f32[16,1024]{1,0:T(8,128)S(1)}, s32[]{:T(128)}, f32[32,16,1024]{2,1,0:T(8,128)}, f32[32,16,1024]{2,1,0:T(8,128)}) %tuple.94), condition=%wide.region_5.6_spmd.clone.clone, body=%wide.region_4.5_spmd.clone.sunk.clone | while | flops 65540 | bytes 262237 | solution.py:27
  230.2 71.4 %while.28 = (s32[]{:T(128)}, f32[16,1024]{1,0:T(8,128)S(1)}, f32[64,1024]{1,0:T(8,128)S(1)}, f32[64,16,1024]{2,1,0:T(8,128)}, f32[64,16,1024]{2,1,0:T(8,128)}, /*index=5*/f32[64,16]{1,0:T(8,128)S(1)}) while((s32[]{:T(128)}, f32[16,1024]{1,0:T(8,128)S(1)}, f32[64,1024]{1,0:T(8,128)S(1)}, f32[64,16,1024]{2,1,0:T(8,128)}, ...), condition=%wide.region_8.9_spmd.clone, body=%wide.region_6.8_spmd.sunk.clone | while | flops 64514 | bytes 274713 | solution.py:92
  301.6 2.9 all-gather.6.cloned.1.call-done
  304.6 6.1 fusion.18
  311.1 32.4 %reduce-scatter.3.cloned.1.call-done = f32[8,4096]{1,0:T(8,128)} async-done(((f32[64,4096]{1,0:T(8,128)}), f32[8,4096]{1,0:T(8,128)}) %reduce-scatter.3.cloned.1.call-update) | async-done | bytes 131088 | tf_op jit(solution)/shard_map/reduce_scatter | solution.py:101
  346.1 12.1 %all_to_all.28 = bf16[8,4,4096]{2,1,0:T(4,128)(2,1)S(1)} all-to-all(bf16[8,4,4096]{2,1,0:T(4,128)(2,1)S(1)} %all_to_all.18), channel_id=1, replica_groups=mesh['seq'=32,'exp'=8] {'exp'}, dimensions={0} | all-to-all | bytes 524288 | tf_op jit(solution)/shard_map/all_to_all | solution.py:123
  358.2 5.2 collective-permute-start.1
  363.4 4.6 collective-permute-done.1
  368.0 2.6 collective-permute-start.2
  370.6 10.5 %collective-permute-done.2 = bf16[64,4096]{1,0:T(8,128)(2,1)S(1)} collective-permute-done((bf16[64,4096]{1,0:T(8,128)(2,1)S(1)}, bf16[64,4096]{1,0:T(8,128)(2,1)S(1)}, u32[]{:S(2)}, u32[]{:S(2)}) %collective-permute-start.2) | collective-permute-done | bytes 524320 | tf_op jit(solution)/shard_map/ppermute | solution.py:131
  382.3 20.7 %collective-permute-done.3 = bf16[128,4096]{1,0:T(8,128)(2,1)S(1)} collective-permute-done((bf16[128,4096]{1,0:T(8,128)(2,1)S(1)}, bf16[128,4096]{1,0:T(8,128)(2,1)S(1)}, u32[]{:S(2)}, u32[]{:S(2)}) %collective-permute-start.3) | collective-permute-done | bytes 1048608 | tf_op jit(solution)/shard_map/ppermute | solution.py:131
  403.2 2.0 collective-permute-start.4
  407.9 1.6 constant_dynamic-update-slice_fusion.1
  409.5 57.9 %collective-permute-done.4 = bf16[256,4096]{1,0:T(8,128)(2,1)S(1)} collective-permute-done((bf16[256,4096]{1,0:T(8,128)(2,1)S(1)}, bf16[256,4096]{1,0:T(8,128)(2,1)S(1)}, u32[]{:S(2)}, u32[]{:S(2)}) %collective-permute-start.4) | collective-permute-done | bytes 2097184 | tf_op jit(solution)/shard_map/ppermute | solution.py:131
  468.8 2.5 constant_dynamic-update-slice_fusion
  471.3 4.5 collective-permute-start.5
  475.8 181.5 %collective-permute-done.5 = bf16[512,4096]{1,0:T(8,128)(2,1)} collective-permute-done((bf16[512,4096]{1,0:T(8,128)(2,1)}, bf16[512,4096]{1,0:T(8,128)(2,1)}, u32[]{:S(2)}, u32[]{:S(2)}) %collective-permute-start.5) | collective-permute-done | bytes 4194336 | tf_op jit(solution)/shard_map/ppermute | solution.py:131
  657.3 4.7 constant_dynamic-update-slice_fusion.11
  665.4 1.5 constant_dynamic-update-slice_fusion.6
  666.8 4.8 constant_dynamic-update-slice_fusion.5
  671.6 7.7 fusion.2
  679.3 15.6 %convolution_convert_fusion = bf16[1024,4096]{1,0:T(8,128)(2,1)} fusion(bf16[1,448,4096]{2,1,0:T(8,128)(2,1)} %param.38, f32[1024,448]{0,1:T(8,128)} %fusion.2, bf16[2048,4096]{1,0:T(8,128)(2,1)} %constant_dynamic-update-slice_fusion.5, s32[]{:T(128)S(6)} %select_n.64, bf16[1,4096,448]{1,2,0:T(8,128)(2,1)} %param.36), kind=kOutput, calls=%fused_computation.9 | convolution fusion | flops 7523139584 | bytes 25952260 | tf_op jit(solution)/shard_map/dot_general | solution.py:139
  695.2 255.0 %reduce-scatter.5.cloned.1.call-done = bf16[32,4096]{1,0:T(8,128)(2,1)} async-done(((bf16[1024,4096]{1,0:T(8,128)(2,1)}), bf16[32,4096]{1,0:T(8,128)(2,1)}) %reduce-scatter.5.cloned.1.call-update) | async-done | bytes 262160 | tf_op jit(solution)/shard_map/reduce_scatter | solution.py:138
  950.2 1.9 reshape.112
  952.1 8.8 all-to-all-start.1
  961.4 9.0 all-to-all-done.1
  (314 shorter events, 121.1 us)
Async XLA Ops:
  7.2 33.3 %copy-start = (bf16[256,1024]{1,0:T(8,128)(2,1)S(1)}, bf16[256,1024]{1,0:T(8,128)(2,1)}, u32[]{:S(2)}) copy-start(bf16[256,1024]{1,0:T(8,128)(2,1)} %param.28) | copy-start | bytes 1572868
  7.2 114.7 %all-gather.8.cloned.1.call-start = ((), (), s32[]{:S(2)}) async-start(), calls=%async_computation.7 | async-start | bytes 2162688 | tf_op jit(solution)/shard_map/all_gather | solution.py:15
  8.0 4.8 collective-permute-start
  43.2 157.0 %all-gather.10.cloned.1.call-start = ((), (), s32[]{:S(2)}) async-start(), calls=%async_computation.8 | async-start | bytes 2162688 | tf_op jit(solution)/shard_map/all_gather | solution.py:15
  43.4 261.2 %copy-start.7 = (bf16[64,1024]{1,0:T(8,128)(2,1)S(1)}, bf16[64,1024]{1,0:T(8,128)(2,1)}, u32[]{:S(2)}) copy-start(bf16[64,1024]{1,0:T(8,128)(2,1)} %param.23) | copy-start | bytes 393220
  43.4 261.1 %copy-start.9 = (f32[1024]{0:T(1024)S(1)}, f32[1024]{0:T(1024)}, u32[]{:S(2)}) copy-start(f32[1024]{0:T(1024)} %param.31) | copy-start | bytes 12292
  47.8 256.8 %all-gather.6.cloned.1.call-start = ((), (), s32[]{:S(2)}) async-start(), calls=%async_computation.4 | async-start | bytes 8650752 | tf_op jit(solution)/shard_map/all_gather | solution.py:98
  48.5 295.0 %reduce-scatter.3.cloned.1.call-start = ((), (), s32[]{:S(2)}) async-start(), calls=%async_computation.5 | async-start | bytes 1179648 | tf_op jit(solution)/shard_map/reduce_scatter | solution.py:101
  304.6 6.2 copy-start.11
  304.6 39.0 %copy-start.5 = (bf16[8,4096]{1,0:T(8,128)(2,1)S(1)}, bf16[8,4096]{1,0:T(8,128)(2,1)}, u32[]{:S(2)}) copy-start(bf16[8,4096]{1,0:T(8,128)(2,1)} %param.33) | copy-start | bytes 196612
  304.6 40.0 %copy-start.10 = (f32[4096]{0:T(1024)S(1)}, f32[4096]{0:T(1024)}, u32[]{:S(2)}) copy-start(f32[4096]{0:T(1024)} %param.34) | copy-start | bytes 49156
  310.7 639.5 %reduce-scatter.5.cloned.1.call-start = ((), (), s32[]{:S(2)}) async-start(), calls=%async_computation.6 | async-start | bytes 8650752 | tf_op jit(solution)/shard_map/reduce_scatter | solution.py:138
  358.2 9.8 collective-permute-start.1
  368.0 13.0 %collective-permute-start.2 = (bf16[64,4096]{1,0:T(8,128)(2,1)S(1)}, bf16[64,4096]{1,0:T(8,128)(2,1)S(1)}, u32[]{:S(2)}, u32[]{:S(2)}) collective-permute-start(bf16[64,4096]{1,0:T(8,128)(2,1)S(1)} %pad_maximum_fusion.2), channel_id=1, source_target_pairs={{0,240},{8,248},{16,0},{24,8},{32,16},{40,24},{48,32},{56,40},{64,... | collective-permute-start | bytes 1572872 | tf_op jit(solution)/shard_map/ppermute | solution.py:131
  381.1 21.8 %collective-permute-start.3 = (bf16[128,4096]{1,0:T(8,128)(2,1)S(1)}, bf16[128,4096]{1,0:T(8,128)(2,1)S(1)}, u32[]{:S(2)}, u32[]{:S(2)}) collective-permute-start(bf16[128,4096]{1,0:T(8,128)(2,1)S(1)} %pad_maximum_fusion.1), channel_id=1, source_target_pairs={{0,224},{8,232},{16,240},{24,248},{32,0},{40,8},{48,16},{56,24},{6... | collective-permute-start | bytes 3145736 | tf_op jit(solution)/shard_map/ppermute | solution.py:131
  403.2 64.2 %collective-permute-start.4 = (bf16[256,4096]{1,0:T(8,128)(2,1)S(1)}, bf16[256,4096]{1,0:T(8,128)(2,1)S(1)}, u32[]{:S(2)}, u32[]{:S(2)}) collective-permute-start(bf16[256,4096]{1,0:T(8,128)(2,1)S(1)} %pad_maximum_fusion), channel_id=1, source_target_pairs={{0,192},{8,200},{16,208},{24,216},{32,224},{40,232},{48,240},{56,2... | collective-permute-start | bytes 6291464 | tf_op jit(solution)/shard_map/ppermute | solution.py:131
  467.4 1.4 copy-start.2
  471.3 186.0 %collective-permute-start.5 = (bf16[512,4096]{1,0:T(8,128)(2,1)}, bf16[512,4096]{1,0:T(8,128)(2,1)}, u32[]{:S(2)}, u32[]{:S(2)}) collective-permute-start(bf16[512,4096]{1,0:T(8,128)(2,1)} %get-tuple-element.192), channel_id=1, source_target_pairs={{0,128},{8,136},{16,144},{24,152},{32,160},{40,168},{48,176},{56,1... | collective-permute-start | bytes 12582920 | tf_op jit(solution)/shard_map/ppermute | solution.py:131
  662.0 3.4 copy-start.3
  666.8 4.8 copy-start.12
  694.9 266.0 %copy-start.8 = (f32[4096,8]{0,1:T(8,128)S(1)}, f32[4096,8]{0,1:T(8,128)}, u32[]{:S(2)}) copy-start(f32[4096,8]{0,1:T(8,128)} %param.35) | copy-start | bytes 393220
  695.0 276.9 %copy-start.4 = (f32[8,4096]{1,0:T(8,128)S(1)}, f32[8,4096]{1,0:T(8,128)}, u32[]{:S(2)}) copy-start(f32[8,4096]{1,0:T(8,128)} %reduce-scatter.3.cloned.1.call-done) | copy-start | bytes 393220
  695.0 277.5 %copy-start.1 = (bf16[256,1024]{1,0:T(8,128)(2,1)S(1)}, bf16[256,1024]{1,0:T(8,128)(2,1)}, u32[]{:S(2)}) copy-start(bf16[256,1024]{1,0:T(8,128)(2,1)} %param.28) | copy-start | bytes 1572868
  952.1 18.3 %all-to-all-start.1 = ((f32[8,4,4096]{2,1,0:T(4,128)}), f32[8,4,4096]{2,1,0:T(4,128)S(1)}, u32[]{:S(2)}, u32[]{:S(2)}) async-start(f32[8,4,4096]{2,1,0:T(4,128)} %reshape.112), calls=%async_computation.3 | async-start | bytes 1048576 | tf_op jit(solution)/shard_map/all_to_all | solution.py:144
  971.8 0.7 copy-start.6
Sparse Core Ops, SparseCore 0:
  43.4 78.4 all-gather.7
  125.1 75.1 all-gather.9
  202.7 101.8 all-gather.5
  310.8 32.6 reduce-scatter.2
  695.1 255.0 reduce-scatter.4
